TPU v7x, 128 devices: a whole 4x4x4 slice. The times are simulated.
128 devices in a mesh: gz: 8 (over x, z_hi), ta: 16 (over y, z_lo, core).
Axes of the slice: x: 4, y: 4, z: 4 (z_hi: 2, z_lo: 2; z = z_hi * 2 + z_lo), core: 2. Of those that a mesh axis runs over, the one named last changes fastest.
Arguments:
- source: float32 [24, 32, 128, 128], P(None, 'gz', 'ta'), may hold values from -6 to 6
- gauge_links: float32 [4, 18, 32, 128, 128], P(None, None, 'gz', 'ta'), may hold values from -2.5 to 2.5
- clover_term: float32 [2, 2, 6, 6, 32, 128, 128], P(None, None, None, None, 'gz', 'ta'), may hold values from -0.9 to 0.9
- null_vectors: bfloat16 [24, 24, 32, 128, 128], P(None, None, 'gz', 'ta'), may hold values from -0.109375 to 0.109375
- owners: int32 [2048, 1], P(('gz', 'ta')), may hold values from 0 to 15; in each aligned block of 16 rows (0 to 15, 16 to 31, ...) at most 2 rows name the same one
Outputs:
- solution: float32 [24, 32, 128, 128], P(None, 'gz', 'ta')
- coarse: float32 [96, 4096], P(None, ('gz', 'ta'))
Inputs may be any that keep to these rules, and one draw needn't show every extreme that they name: `owners`: in each aligned block of 16 rows no owner is named more than 2 times, and in some block one owner is named exactly that often.
All inputs are finite; a program needn't handle non-finite values.
Results may differ from a plain program's by a relative error of at most 0.0029.
Values sent between devices are 32-bit elements; how exact they have to be, the bound alone decides.
A program may use at most 128 MiB of HBM per device.

v0:
```python
import jax
import jax.numpy as jnp
from jax import lax
from jax.experimental import pallas as pl
from jax.experimental.pallas import tpu as pltpu
from jax.sharding import PartitionSpec as P

MESH = pl.DeviceIdType.MESH
F32 = jnp.float32
BF16 = jnp.bfloat16

NZ = 4
COMPS = 24
VECS = 24
GZ = 8
TA = 16
PLANE = 32
FIELD = COMPS * PLANE
WEIGHT = 0.24
MASS = 4.2
HALF = 0.5 * WEIGHT
KAPPA = 2.0 / WEIGHT - 2.0 * MASS
X, Y, Z, T = 0, 1, 2, 3

SPIN = {
    X: [[(-1, 1, 1), (-1, 1, 0)], [(1, 0, 1), (1, 0, 0)]],
    Y: [[(1, 0, 1), (-1, 0, 0)], [(1, 1, 1), (-1, 1, 0)]],
    Z: [[(-1, 1, 0), (1, 1, 1)], [(1, 0, 0), (-1, 0, 1)]],
    T: [[(-1, 0, 0), (-1, 0, 1)], [(-1, 1, 0), (-1, 1, 1)]],
}
INVERSE = {X: -1, Y: -1, Z: -1, T: 1}


def comp(reim, spin, colour):
    return 12 * reim + 3 * spin + colour


def half(reim, spin, colour):
    return 6 * reim + 3 * spin + colour


def add(a, b, sign):
    return a + b if sign > 0 else a - b


def project(load, direction, parity, s):
    out = []
    for r in range(2):
        sign, r2, s2 = SPIN[direction][r][s]
        out.append([add(load(r, s, c), load(r2, 2 + s2, c), -parity * sign) for c in range(3)])
    return out


def colour(link, a, dagger):
    re, im = [], []
    for row in range(3):
        tr = ti = None
        for k in range(3):
            e = 3 * k + row if dagger else 3 * row + k
            lr, li = link[e], link[9 + e]
            if dagger:
                nr = lr * a[0][k] + li * a[1][k]
                ni = lr * a[1][k] - li * a[0][k]
            else:
                nr = lr * a[0][k] - li * a[1][k]
                ni = lr * a[1][k] + li * a[0][k]
            tr = nr if tr is None else tr + nr
            ti = ni if ti is None else ti + ni
        re.append(tr)
        im.append(ti)
    return [re, im]


def lower_terms(direction, s):
    out = []
    for r in range(2):
        for spin in range(2):
            sign, r2, s2 = SPIN[direction][r][spin]
            if s2 == s:
                out.append((INVERSE[direction] * sign, r2, r, 2 + spin))
    return out


def kernel(
    source, links, clover, vectors, owners, x_out, coarse_out,
    y, g, cl, v, sz, st, sr, sl, rz, rt, rd, rl, tmp, wt, place, so, rc, xs,
    load_sem, msg_send, msg_recv, diag_send, diag_recv, link_send, link_recv, all_send, all_recv, x_sem,
):
    me_z = lax.axis_index("gz")
    me_t = lax.axis_index("ta")

    def device(dz, dt):
        return (lax.rem(me_z + (dz + GZ), GZ), lax.rem(me_t + (dt + TA), TA))

    loads = [
        pltpu.make_async_copy(source, y.at[pl.ds(0, FIELD)], load_sem.at[0]),
        pltpu.make_async_copy(links, g, load_sem.at[1]),
        pltpu.make_async_copy(clover, cl, load_sem.at[2]),
        pltpu.make_async_copy(vectors, v, load_sem.at[3]),
    ]
    for c in loads:
        c.start()

    barrier = pltpu.get_barrier_semaphore()
    greet = [(dz, dt) for dz in (-1, 1) for dt in (-1, 0, 1)] + [(0, dt) for dt in range(1, TA)]
    for dz, dt in greet:
        pl.semaphore_signal(barrier, inc=1, device_id=device(dz, dt), device_id_type=MESH)

    down_sign = jnp.where(me_t == 0, -1.0, 1.0).astype(F32)
    up_sign = jnp.where(me_t == TA - 1, -1.0, 1.0).astype(F32)

    sub = lax.broadcasted_iota(jnp.int32, (16, 128), 0)
    lane = lax.broadcasted_iota(jnp.int32, (16, 128), 1)
    own = jnp.broadcast_to(owners[...].astype(F32), (16, 128))
    own_row = jnp.sum(jnp.where(sub == lane, own, 0.0), axis=0, keepdims=True)
    rank = jnp.sum(jnp.where((own == own_row) & (lane < sub), 1.0, 0.0), axis=1, keepdims=True)
    slot = own * 8.0 + rank
    for part in range(2):
        agg = ((lane & 7) >> 2) * 8 + ((lane >> 4) & 7)
        of_lane = jnp.sum(jnp.where(agg == sub, slot, 0.0), axis=0, keepdims=True)
        row = lax.broadcasted_iota(jnp.int32, (128, 128), 0).astype(F32)
        place[:, 128 * part:128 * (part + 1)] = jnp.where(row == of_lane, 1.0, 0.0)

    for j in (0, 2, 4, 6, 8, 9, 12, 13):
        for e in (0, 8, 16):
            diag = lax.broadcasted_iota(jnp.int32, (8, 128), 0) + e
            rl[pl.ds(24 * j + e, 8), :] = jnp.where(
                (diag == 0) | (diag == 4) | (diag == 8), jnp.ones((8, 128), F32), 0.0
            )

    def yrow(k, c, z, t=0):
        return k * FIELD + c * PLANE + z * 8 + t

    def y_at(k, z):
        def load(r, s, c):
            return y[pl.ds(pl.multiple_of(yrow(k, comp(r, s, c), z), 8), 8), :]
        return load

    def link_at(direction, z):
        return [
            g[pl.ds(pl.multiple_of((18 * direction + e) * PLANE + z * 8, 8), 8), :]
            for e in range(18)
        ]

    def bump(k, z, r, s, c, value, sign=1):
        at = pl.ds(pl.multiple_of(yrow(k, comp(r, s, c), z), 8), 8)
        y[at, :] = add(y[at, :], value, sign)

    y_lane = lax.broadcasted_iota(jnp.int32, (8, 128), 1) & 15
    t_row = lax.broadcasted_iota(jnp.int32, (8, 128), 0)

    def ahead(direction, a):
        if direction == X:
            return pltpu.roll(a, 112, 1)
        if direction == Y:
            return jnp.where(y_lane == 15, pltpu.roll(a, 15, 1), pltpu.roll(a, 127, 1))
        return jnp.where(t_row == 7, 0.0, pltpu.roll(a, 7, 0))

    def behind(direction, a):
        if direction == X:
            return pltpu.roll(a, 16, 1)
        if direction == Y:
            return jnp.where(y_lane == 0, pltpu.roll(a, 113, 1), pltpu.roll(a, 1, 1))
        return jnp.where(t_row == 0, 0.0, pltpu.roll(a, 1, 0))

    def layer(k, z):
        load = y_at(k, z)
        for h in range(2):
            vr = [load(0, 2 * h + i // 3, i % 3) for i in range(6)]
            vi = [load(1, 2 * h + i // 3, i % 3) for i in range(6)]
            ur = [-2.0 * a for a in vr]
            ui = [-2.0 * a for a in vi]
            for row in range(6):
                tr = KAPPA * vr[row]
                ti = KAPPA * vi[row]
                for k2 in range(6):
                    base = ((2 * h) * 6 + row) * 6 + k2
                    cr = cl[pl.ds(pl.multiple_of(base * PLANE + z * 8, 8), 8), :]
                    ci = cl[pl.ds(pl.multiple_of((base + 36) * PLANE + z * 8, 8), 8), :]
                    tr = tr + (cr * ur[k2] - ci * ui[k2])
                    ti = ti + (cr * ui[k2] + ci * ur[k2])
                s, c = 2 * h + row // 3, row % 3
                y[pl.ds(pl.multiple_of(yrow(k + 1, comp(0, s, c), z), 8), 8), :] = tr
                y[pl.ds(pl.multiple_of(yrow(k + 1, comp(1, s, c), z), 8), 8), :] = ti
        for direction in (X, Y, T):
            link = link_at(direction, z)
            for s in range(2):
                fwd = project(load, direction, -1, s)
                fwd = [[ahead(direction, a) for a in part] for part in fwd]
                fwd = colour(link, fwd, False)
                bwd = colour(link, project(load, direction, 1, s), True)
                bwd = [[behind(direction, a) for a in part] for part in bwd]
                for r in range(2):
                    for c in range(3):
                        bump(k + 1, z, r, s, c, fwd[r][c] + bwd[r][c])
                for sign, r2, r, s2 in lower_terms(direction, s):
                    for c in range(3):
                        bump(k + 1, z, r, s2, c, fwd[r2][c] - bwd[r2][c], sign)

    def z_link(k, z):
        link = link_at(Z, z)
        for s in range(2):
            fwd = colour(link, project(y_at(k, z + 1), Z, -1, s), False)
            put_half(k + 1, z, s, fwd, 1)
            bwd = colour(link, project(y_at(k, z), Z, 1, s), True)
            put_half(k + 1, z + 1, s, bwd, -1)

    def put_half(k, z, s, w, parity):
        for r in range(2):
            for c in range(3):
                bump(k, z, r, s, c, w[r][c])
        for sign, r2, r, s2 in lower_terms(Z, s):
            for c in range(3):
                bump(k, z, r, s2, c, w[r2][c], parity * sign)

    def local(k, at_third):
        def step(i, carry):
            z = lax.rem(i + 1, NZ)
            if at_third is not None:
                @pl.when(i == 2)
                def _():
                    at_third()
            layer(k, z)

            @pl.when(i > 0)
            def _():
                z_link(k, lax.rem(i, 3))
            return carry
        lax.fori_loop(0, NZ, step, 0)

    def rows_of(k, t):
        def load(r, s, c):
            return y[pl.ds(yrow(k, comp(r, s, c), 0, t), NZ, stride=8), :]
        return load

    def link_rows(t):
        return [g[pl.ds((18 * T + e) * PLANE + t, NZ, stride=8), :] for e in range(18)]

    def pack(k):
        link = link_at(Z, NZ - 1)
        tlink = link_rows(7)
        for s in range(2):
            dn = project(y_at(k, 0), Z, -1, s)
            up = colour(link, project(y_at(k, NZ - 1), Z, 1, s), True)
            for r in range(2):
                for c in range(3):
                    sz[k, 0, pl.ds(8 * half(r, s, c), 8), :] = dn[r][c]
                    sz[k, 1, pl.ds(8 * half(r, s, c), 8), :] = up[r][c]
            dn = project(rows_of(k, 0), T, -1, s)
            up = colour(tlink, project(rows_of(k, 7), T, 1, s), True)
            for r in range(2):
                for c in range(3):
                    at = pl.ds(8 * r + 3 * s + c, NZ, stride=16)
                    st[k, 0, at, :] = dn[r][c] * down_sign
                    st[k, 1, at, :] = up[r][c] * up_sign

    def pack_corners(p, k):
        for m in range(2):
            for i, (t, sign) in enumerate(((0, down_sign), (7, up_sign))):
                for r in range(2):
                    rows = sz[k, m, pl.ds(48 * r + t, 6, stride=8), :]
                    sr[p, 2 * m + i, pl.ds(8 * r, 6), :] = rows * sign

    def message(k, m):
        target = ((-1, 0), (1, 0), (0, -1), (0, 1))[m]
        src, dst = (sz, rz) if m < 2 else (st, rt)
        return pltpu.make_async_remote_copy(
            src_ref=src.at[k, m % 2], dst_ref=dst.at[k, m % 2],
            send_sem=msg_send.at[k, m], recv_sem=msg_recv.at[k, m],
            device_id=device(*target), device_id_type=MESH,
        )

    def corner(p, k, j):
        src = (
            st.at[k, 1, pl.ds(0, 16)], st.at[k, 0, pl.ds(0, 16)],
            st.at[k, 1, pl.ds(48, 16)], st.at[k, 0, pl.ds(48, 16)],
            sr.at[p, 2], sr.at[p, 0], sr.at[p, 3], sr.at[p, 1],
        )[j]
        target = ((-1, 1), (-1, -1), (1, 1), (1, -1), (1, -1), (-1, -1), (1, 1), (-1, 1))[j]
        return pltpu.make_async_remote_copy(
            src_ref=src, dst_ref=rd.at[p, pl.ds(16 * j, 16)],
            send_sem=diag_send.at[p, j], recv_sem=diag_recv.at[p, j],
            device_id=device(*target), device_id_type=MESH,
        )

    def corner_link(i):
        block, target, to = (
            (0, (-1, 0), 1), (1, (1, 0), 3), (2, (1, 0), 10), (3, (1, 0), 11),
            (2, (0, -1), 5), (3, (0, 1), 7), (0, (0, 1), 14), (1, (0, 1), 15),
        )[i]
        return pltpu.make_async_remote_copy(
            src_ref=sl.at[block], dst_ref=rl.at[pl.ds(24 * to, 24)],
            send_sem=link_send.at[i], recv_sem=link_recv.at[i],
            device_id=device(*target), device_id_type=MESH,
        )

    def finish_t(k):
        link = link_rows(7)
        for s in range(2):
            a = [[rt[k, 0, pl.ds(8 * r + 3 * s + c, NZ, stride=16), :] for c in range(3)] for r in range(2)]
            b = [[rt[k, 1, pl.ds(8 * r + 3 * s + c, NZ, stride=16), :] for c in range(3)] for r in range(2)]
            for w, t, parity in ((colour(link, a, False), 7, 1), (b, 0, -1)):
                def bump_row(r, s, c, value, sign):
                    at = pl.ds(yrow(k + 1, comp(r, s, c), 0, t), NZ, stride=8)
                    y[at, :] = add(y[at, :], value, sign)
                for r in range(2):
                    for c in range(3):
                        bump_row(r, s, c, w[r][c], 1)
                for sign, r2, r, s2 in lower_terms(T, s):
                    for c in range(3):
                        bump_row(r, s2, c, w[r2][c], parity * sign)

    def finish_z(k):
        link = link_at(Z, NZ - 1)
        for s in range(2):
            a = [[rz[k, 0, pl.ds(8 * half(r, s, c), 8), :] for c in range(3)] for r in range(2)]
            put_half(k + 1, NZ - 1, s, colour(link, a, False), 1)
            b = [[rz[k, 1, pl.ds(8 * half(r, s, c), 8), :] for c in range(3)] for r in range(2)]
            put_half(k + 1, 0, s, b, -1)

    def correct(p, k):
        one = [rl[pl.ds(e, 8, stride=24), :] for e in range(18)]
        two = [rl[pl.ds(192 + e, 8, stride=24), :] for e in range(18)]
        j = lax.broadcasted_iota(jnp.int32, (8, 128), 0)
        plus = (j == 0) | (j == 3) | (j == 5) | (j == 6)
        sign_j = jnp.where(plus, jnp.ones((8, 128), F32), -1.0)
        w = []
        for s in range(2):
            a = [[rd[p, pl.ds(8 * r + 3 * s + c, 8, stride=16), :] for c in range(3)] for r in range(2)]
            w.append(colour(one, a, False))
        for s in range(2):
            q = []
            for r in range(2):
                sign, r2, s2 = SPIN[Z][r][s]
                q.append([add(w[s][r][c], sign_j * w[s2][r2][c], sign) for c in range(3)])
            q = colour(two, q, True)
            for r in range(2):
                for c in range(3):
                    tmp[pl.ds(8 * half(r, s, c), 8), :] = q[r][c]
        for s in range(2):
            for r in range(2):
                for c in range(3):
                    n = half(r, s, c)
                    for m in range(2):
                        at = pl.ds(8 * n, 2, stride=7)
                        rz[k, m, at, :] = rz[k, m, at, :] + tmp[pl.ds(8 * n + 2 * m, 2), :]
                        at = pl.ds(8 * r + 3 * s + c, 2, stride=48)
                        rt[k, m, at, :] = rt[k, m, at, :] + tmp[pl.ds(8 * n + 4 + 2 * m, 2), :]

    loads[0].wait()
    loads[1].wait()
    for i, (direction, z, t) in enumerate(((T, 0, 7), (T, 3, 7), (Z, 3, 0), (Z, 3, 7))):
        for e, count in ((0, 8), (8, 8), (16, 2)):
            sl[i, pl.ds(e, count), :] = g[pl.ds((18 * direction + e) * PLANE + z * 8 + t, count, stride=32), :]
    loads[2].wait()
    pl.semaphore_wait(barrier, len(greet))

    for p in range(2):
        k = 2 * p
        pack(k)
        for m in range(4):
            message(k, m).start()
        pack_corners(p, k)
        for j in range(8):
            corner(p, k, j).start()
        if p == 0:
            for i in range(8):
                corner_link(i).start()
        local(k, None)
        pack(k + 1)
        for m in range(4):
            message(k + 1, m).start()
        message(k, 2).wait_recv()
        message(k, 3).wait_recv()
        finish_t(k)

        def at_third():
            message(k, 0).wait_recv()
            message(k, 1).wait_recv()
            finish_z(k)
        local(k + 1, at_third)
        for j in range(8):
            corner(p, k, j).wait_recv()
        if p == 0:
            for i in range(8):
                corner_link(i).wait_recv()
        for m in range(4):
            message(k + 1, m).wait_recv()
        correct(p, k + 1)
        finish_t(k + 1)
        finish_z(k + 1)

    loads[3].wait()
    site = lax.broadcasted_iota(jnp.int32, (16, 128), 1)
    group = (site >> 6) * 4 + ((site & 15) >> 2)
    scale = HALF ** 4
    pooled = []
    for h in range(2):
        left = []
        for zp in range(2):
            for c in range(6):
                rows = []
                for r in range(2):
                    n = comp(r, 2 * h, 0) + c
                    rows.append((y[pl.ds(yrow(4, n, 2 * zp), 16), :] * scale).astype(BF16))
                    left.append(v[:, pl.ds(n * PLANE + 16 * zp, 16), :].reshape(VECS * 16, 128))
                col = (zp * 6 + c) * 256
                for grp in range(8):
                    keep = (group == grp).astype(F32).astype(BF16)
                    re, im = rows[0] * keep, rows[1] * keep
                    wt[pl.ds(16 * grp, 16), col:col + 128] = re
                    wt[pl.ds(16 * grp, 16), col + 128:col + 256] = im
                    wt[pl.ds(128 + 16 * grp, 16), col:col + 128] = im
                    wt[pl.ds(128 + 16 * grp, 16), col + 128:col + 256] = -re
        prod = lax.dot_general(
            jnp.concatenate(left, axis=1), wt[...], (((1,), (1,)), ((), ())), preferred_element_type=F32
        )
        i0 = lax.broadcasted_iota(jnp.int32, (VECS * 16, 256), 0) & 15
        i1 = lax.broadcasted_iota(jnp.int32, (VECS * 16, 256), 1) & 15
        prod = jnp.where(i0 == i1, prod, 0.0)
        pooled.append(jnp.sum(prod.reshape(VECS, 16, 256), axis=1))
    zero = jnp.zeros((2 * VECS, 128), F32)
    pooled = jnp.concatenate(pooled, axis=0)
    first = jnp.concatenate([pooled[:, :128], zero], axis=1)
    second = jnp.concatenate([zero, pooled[:, 128:]], axis=1)
    values = jnp.concatenate([first, second, jnp.zeros((32, 256), F32)], axis=0)
    so[...] = lax.dot_general(
        place[...], values, (((1,), (1,)), ((), ())), preferred_element_type=F32,
        precision=lax.Precision.HIGHEST,
    )

    def exchange(d):
        to = lax.rem(me_t + d, TA)
        return pltpu.make_async_remote_copy(
            src_ref=so.at[pl.ds(pl.multiple_of(8 * to, 8), 8)],
            dst_ref=rc.at[pl.ds(pl.multiple_of(8 * me_t, 8), 8)],
            send_sem=all_send.at[d], recv_sem=all_recv.at[d],
            device_id=(me_z, to), device_id_type=MESH,
        )

    for d in range(1, TA):
        exchange(d).start()
    mine = pl.ds(pl.multiple_of(8 * me_t, 8), 8)
    rc[mine, :] = so[mine, :]

    def solution_rows(i, carry):
        at = [pl.ds(pl.multiple_of(n * FIELD + i * 32, 8), 32) for n in range(4)]
        total = y[at[2], :] + HALF * y[at[3], :]
        total = y[at[1], :] + HALF * total
        total = y[at[0], :] + HALF * total
        xs[at[0], :] = WEIGHT * total
        return carry
    lax.fori_loop(0, COMPS, solution_rows, 0)
    write = pltpu.make_async_copy(xs, x_out, x_sem)
    write.start()

    for d in range(1, TA):
        exchange(d).wait()
    coarse_out[...] = rc[...]
    for p in range(2):
        for m in range(4):
            message(2 * p, m).wait_send()
            message(2 * p + 1, m).wait_send()
        for j in range(8):
            corner(p, 2 * p, j).wait_send()
    for i in range(8):
        corner_link(i).wait_send()
    write.wait()


def on_device(source, gauge_links, clover_term, null_vectors, owners):
    any_space = pl.BlockSpec(memory_space=pl.ANY)
    vmem = pl.BlockSpec(memory_space=pltpu.VMEM)
    dma = pltpu.SemaphoreType.DMA
    x, coarse = pl.pallas_call(
        kernel,
        out_shape=(jax.ShapeDtypeStruct((FIELD, 128), F32), jax.ShapeDtypeStruct((128, 128), F32)),
        in_specs=[any_space, any_space, any_space, any_space, vmem],
        out_specs=(any_space, vmem),
        scratch_shapes=[
            pltpu.VMEM((5 * FIELD, 128), F32),
            pltpu.VMEM((72 * PLANE, 128), F32),
            pltpu.VMEM((144 * PLANE, 128), F32),
            pltpu.VMEM((VECS, FIELD, 128), BF16),
            pltpu.VMEM((4, 2, 96, 128), F32),
            pltpu.VMEM((4, 2, 64, 128), F32),
            pltpu.VMEM((2, 4, 16, 128), F32),
            pltpu.VMEM((4, 24, 128), F32),
            pltpu.VMEM((4, 2, 96, 128), F32),
            pltpu.VMEM((4, 2, 64, 128), F32),
            pltpu.VMEM((2, 128, 128), F32),
            pltpu.VMEM((16 * 24, 128), F32),
            pltpu.VMEM((96, 128), F32),
            pltpu.VMEM((256, 3072), BF16),
            pltpu.VMEM((128, 256), F32),
            pltpu.VMEM((128, 128), F32),
            pltpu.VMEM((128, 128), F32),
            pltpu.VMEM((FIELD, 128), F32),
            dma((4,)), dma((4, 4)), dma((4, 4)), dma((2, 8)), dma((2, 8)),
            dma((8,)), dma((8,)), dma((TA,)), dma((TA,)), dma,
        ],
        compiler_params=pltpu.CompilerParams(
            collective_id=0, has_side_effects=True, vmem_limit_bytes=48 * 1024 * 1024
        ),
    )(
        source.reshape(FIELD, 128),
        gauge_links.reshape(72 * PLANE, 128),
        clover_term.reshape(144 * PLANE, 128),
        null_vectors.reshape(VECS, FIELD, 128),
        owners,
    )
    coarse = coarse.reshape(TA, 8, 128)[:, :2, :4 * VECS].reshape(2 * TA, 4 * VECS).T
    return x.reshape(source.shape), coarse


def solution(mesh):
    in_specs = (
        P(None, "gz", "ta", None),
        P(None, None, "gz", "ta", None),
        P(None, None, None, None, "gz", "ta", None),
        P(None, None, "gz", "ta", None),
        P(("gz", "ta"), None),
    )
    out_specs = (P(None, "gz", "ta", None), P(None, ("gz", "ta")))
    return jax.shard_map(
        on_device, mesh=mesh, in_specs=in_specs, out_specs=out_specs, check_vma=False
    )
```

profile of v0, /device:TPU:1, one launch (start us, length us, event | category | flops | bytes accessed | tf_op | source)
XLA Modules:
  0.0 41.1 jit_solution(5113440129670372933)
XLA Ops:
  0.6 0.7 %copy.7.owners = s32[16,1]{1,0:T(8,128)S(1)} copy(s32[16,1]{0,1:T(1,128)} %param.9) | data formatting | bytes 128 | tf_op args[4]
  1.4 0.0 copy-start
  1.4 1.7 %copy-done = f32[2,2,6,6,4,8,128]{6,5,4,3,2,1,0:T(8,128)S(1)} copy-done((f32[2,2,6,6,4,8,128]{6,5,4,3,2,1,0:T(8,128)S(1)}, f32[2,2,6,6,4,8,128]{6,5,4,3,2,1,0:T(8,128)}, u32[]{:S(2)}) %copy-start) | copy-done | bytes 2359320
  3.0 0.0 copy-start.1
  3.0 1.3 %copy-done.1 = f32[4,18,4,8,128]{4,3,2,1,0:T(8,128)S(1)} copy-done((f32[4,18,4,8,128]{4,3,2,1,0:T(8,128)S(1)}, f32[4,18,4,8,128]{4,3,2,1,0:T(8,128)}, u32[]{:S(2)}) %copy-start.1) | copy-done | bytes 1179672
  4.3 0.0 copy-start.2
  4.3 1.0 %copy-done.2 = f32[24,4,8,128]{3,2,1,0:T(8,128)S(1)} copy-done((f32[24,4,8,128]{3,2,1,0:T(8,128)S(1)}, f32[24,4,8,128]{3,2,1,0:T(8,128)}, u32[]{:S(2)}) %copy-start.2) | copy-done | bytes 393240
  5.3 34.5 %shard_map.68 = (f32[768,128]{1,0:T(8,128)S(1)}, f32[128,128]{1,0:T(8,128)S(1)}) custom-call(f32[768,128]{1,0:T(8,128)S(1)} %bitcast.11, f32[2304,128]{1,0:T(8,128)S(1)} %bitcast.10, f32[4608,128]{1,0:T(8,128)S(1)} %bitcast.9, bf16[24,768,128]{2,1,0:T(8,128)(2,1)} %bitcast.14, s32[16,1]{1,0:T(8,128)S(1)} %copy.7.owners), custom_call_target="tpu_custom_call" | custom-call | tf_op jit(solution)/shard_map/pallas_call | solution.py:475
  39.8 0.6 %slice.4 = f32[16,2,96]{2,1,0:T(2,128)} slice(f32[16,8,128]{2,1,0:T(8,128)S(1)} %bitcast.13), slice={[0:16], [0:2], [0:96]} | slice | bytes 24576 | tf_op jit(solution)/shard_map/slice | solution.py:512
  40.4 0.7 %copy.9 = f32[24,4,8,128]{3,2,1,0:T(8,128)} copy(f32[24,4,8,128]{3,2,1,0:T(8,128)S(1)} %bitcast.12) | data formatting | bytes 786432
Async XLA Ops:
  1.4 1.7 %copy-start = (f32[2,2,6,6,4,8,128]{6,5,4,3,2,1,0:T(8,128)S(1)}, f32[2,2,6,6,4,8,128]{6,5,4,3,2,1,0:T(8,128)}, u32[]{:S(2)}) copy-start(f32[2,2,6,6,4,8,128]{6,5,4,3,2,1,0:T(8,128)} %param.7) | copy-start | bytes 7077892
  3.0 1.3 %copy-start.1 = (f32[4,18,4,8,128]{4,3,2,1,0:T(8,128)S(1)}, f32[4,18,4,8,128]{4,3,2,1,0:T(8,128)}, u32[]{:S(2)}) copy-start(f32[4,18,4,8,128]{4,3,2,1,0:T(8,128)} %param.6) | copy-start | bytes 3538948
  4.3 1.0 %copy-start.2 = (f32[24,4,8,128]{3,2,1,0:T(8,128)S(1)}, f32[24,4,8,128]{3,2,1,0:T(8,128)}, u32[]{:S(2)}) copy-start(f32[24,4,8,128]{3,2,1,0:T(8,128)} %param.5) | copy-start | bytes 1179652
where the time goes:
time: 41.4 us; the launch traced here: 41.1 us
  Pallas kernels  34.5 us (83%)
  local copies, waits for them, and re-layouts  6.02 us (15%)
  between operations  0.64 us (2%)
    pallas_call x1, Pallas kernels, on_device(): pl.pallas_call(kernel, out_shape=(jax.ShapeDtypeStruct((FIELD, 128), F32)...  34.5 us
    unnamed x8, local copies, waits for them, and re-layouts  5.41 us

commit v1 on v0

--- a/solution.py
+++ b/solution.py
@@ -28,7 +28,12 @@
     Z: [[(-1, 1, 0), (1, 1, 1)], [(1, 0, 0), (-1, 0, 1)]],
     T: [[(-1, 0, 0), (-1, 0, 1)], [(-1, 1, 0), (-1, 1, 1)]],
 }
+CORNERS = ((-1, 1), (-1, -1), (1, 1), (1, -1))
 INVERSE = {X: -1, Y: -1, Z: -1, T: 1}
+
+
+NEAR_FIRST = (1, 15, 2, 14, 3, 13, 4, 12, 5, 11, 6, 10, 7, 9, 8)
+FAR_FIRST = (8, 7, 9, 6, 10, 5, 11, 4, 12, 3, 13, 2, 14, 1, 15)
 
 
 def comp(reim, spin, colour):
@@ -83,7 +88,7 @@
 
 def kernel(
     source, links, clover, vectors, owners, x_out, coarse_out,
-    y, g, cl, v, sz, st, sr, sl, rz, rt, rd, rl, tmp, wt, place, so, rc, xs,
+    y, g, cl, v, sz, st, sr, sl, ll, rz, rt, rd, rl, tmp, wt, inner, place, so, rc, xs,
     load_sem, msg_send, msg_recv, diag_send, diag_recv, link_send, link_recv, all_send, all_recv, x_sem,
 ):
     me_z = lax.axis_index("gz")
@@ -92,41 +97,45 @@
     def device(dz, dt):
         return (lax.rem(me_z + (dz + GZ), GZ), lax.rem(me_t + (dt + TA), TA))
 
+    def prepare():
+        sub = lax.broadcasted_iota(jnp.int32, (16, 128), 0)
+        lane = lax.broadcasted_iota(jnp.int32, (16, 128), 1)
+        padded = jnp.concatenate([owners[...].astype(F32), jnp.full((1, 112), -1.0, F32)], axis=1)
+        own_row = jnp.broadcast_to(padded, (16, 128))
+        own = jnp.sum(jnp.where(sub == lane, own_row, 0.0), axis=1, keepdims=True)
+        rank = jnp.sum(jnp.where((own == own_row) & (lane < sub), 1.0, 0.0), axis=1, keepdims=True)
+        slot = own * 8.0 + rank
+        for part in range(2):
+            agg = ((lane & 7) >> 2) * 8 + ((lane >> 4) & 7)
+            of_lane = jnp.sum(jnp.where(agg == sub, slot, 0.0), axis=0, keepdims=True)
+            row = lax.broadcasted_iota(jnp.int32, (128, 128), 0).astype(F32)
+            place[:, 128 * part:128 * (part + 1)] = jnp.where(row == of_lane, 1.0, 0.0)
+
+        for j in range(16):
+            for e in (0, 8, 16):
+                diag = lax.broadcasted_iota(jnp.int32, (8, 128), 0) + e
+                rl[pl.ds(24 * j + e, 8), :] = jnp.where(
+                    (diag == 0) | (diag == 4) | (diag == 8), jnp.ones((8, 128), F32), 0.0
+                )
+
+    half_links = 36 * PLANE
     loads = [
         pltpu.make_async_copy(source, y.at[pl.ds(0, FIELD)], load_sem.at[0]),
-        pltpu.make_async_copy(links, g, load_sem.at[1]),
-        pltpu.make_async_copy(clover, cl, load_sem.at[2]),
-        pltpu.make_async_copy(vectors, v, load_sem.at[3]),
+        pltpu.make_async_copy(links.at[pl.ds(half_links, half_links)], g.at[pl.ds(half_links, half_links)], load_sem.at[1]),
+        pltpu.make_async_copy(links.at[pl.ds(0, half_links)], g.at[pl.ds(0, half_links)], load_sem.at[2]),
+        pltpu.make_async_copy(clover, cl, load_sem.at[3]),
+        pltpu.make_async_copy(vectors, v, load_sem.at[4]),
     ]
-    for c in loads:
+    for c in loads[:4]:
         c.start()
 
     barrier = pltpu.get_barrier_semaphore()
-    greet = [(dz, dt) for dz in (-1, 1) for dt in (-1, 0, 1)] + [(0, dt) for dt in range(1, TA)]
+    greet = [(dz, dt) for dz in (-1, 1) for dt in (0, -1, 1)] + [(0, dt) for dt in NEAR_FIRST]
     for dz, dt in greet:
         pl.semaphore_signal(barrier, inc=1, device_id=device(dz, dt), device_id_type=MESH)
 
     down_sign = jnp.where(me_t == 0, -1.0, 1.0).astype(F32)
     up_sign = jnp.where(me_t == TA - 1, -1.0, 1.0).astype(F32)
-
-    sub = lax.broadcasted_iota(jnp.int32, (16, 128), 0)
-    lane = lax.broadcasted_iota(jnp.int32, (16, 128), 1)
-    own = jnp.broadcast_to(owners[...].astype(F32), (16, 128))
-    own_row = jnp.sum(jnp.where(sub == lane, own, 0.0), axis=0, keepdims=True)
-    rank = jnp.sum(jnp.where((own == own_row) & (lane < sub), 1.0, 0.0), axis=1, keepdims=True)
-    slot = own * 8.0 + rank
-    for part in range(2):
-        agg = ((lane & 7) >> 2) * 8 + ((lane >> 4) & 7)
-        of_lane = jnp.sum(jnp.where(agg == sub, slot, 0.0), axis=0, keepdims=True)
-        row = lax.broadcasted_iota(jnp.int32, (128, 128), 0).astype(F32)
-        place[:, 128 * part:128 * (part + 1)] = jnp.where(row == of_lane, 1.0, 0.0)
-
-    for j in (0, 2, 4, 6, 8, 9, 12, 13):
-        for e in (0, 8, 16):
-            diag = lax.broadcasted_iota(jnp.int32, (8, 128), 0) + e
-            rl[pl.ds(24 * j + e, 8), :] = jnp.where(
-                (diag == 0) | (diag == 4) | (diag == 8), jnp.ones((8, 128), F32), 0.0
-            )
 
     def yrow(k, c, z, t=0):
         return k * FIELD + c * PLANE + z * 8 + t
@@ -197,13 +206,15 @@
                     for c in range(3):
                         bump(k + 1, z, r, s2, c, fwd[r2][c] - bwd[r2][c], sign)
 
-    def z_link(k, z):
+    def z_forward(k, z):
         link = link_at(Z, z)
         for s in range(2):
-            fwd = colour(link, project(y_at(k, z + 1), Z, -1, s), False)
-            put_half(k + 1, z, s, fwd, 1)
-            bwd = colour(link, project(y_at(k, z), Z, 1, s), True)
-            put_half(k + 1, z + 1, s, bwd, -1)
+            put_half(k + 1, z, s, colour(link, project(y_at(k, z + 1), Z, -1, s), False), 1)
+
+    def z_backward(k, z):
+        link = link_at(Z, z)
+        for s in range(2):
+            put_half(k + 1, z + 1, s, colour(link, project(y_at(k, z), Z, 1, s), True), -1)
 
     def put_half(k, z, s, w, parity):
         for r in range(2):
@@ -213,18 +224,12 @@
             for c in range(3):
                 bump(k, z, r, s2, c, w[r2][c], parity * sign)
 
-    def local(k, at_third):
+    def local(k, first, at_third):
         def step(i, carry):
-            z = lax.rem(i + 1, NZ)
-            if at_third is not None:
-                @pl.when(i == 2)
-                def _():
-                    at_third()
-            layer(k, z)
-
-            @pl.when(i > 0)
+            @pl.when(i == 2)
             def _():
-                z_link(k, lax.rem(i, 3))
+                at_third()
+            layer(k, lax.rem(i + first, NZ))
             return carry
         lax.fori_loop(0, NZ, step, 0)
 
@@ -236,9 +241,8 @@
     def link_rows(t):
         return [g[pl.ds((18 * T + e) * PLANE + t, NZ, stride=8), :] for e in range(18)]
 
-    def pack(k):
+    def pack_z(k):
         link = link_at(Z, NZ - 1)
-        tlink = link_rows(7)
         for s in range(2):
             dn = project(y_at(k, 0), Z, -1, s)
             up = colour(link, project(y_at(k, NZ - 1), Z, 1, s), True)
@@ -246,20 +250,30 @@
                 for c in range(3):
                     sz[k, 0, pl.ds(8 * half(r, s, c), 8), :] = dn[r][c]
                     sz[k, 1, pl.ds(8 * half(r, s, c), 8), :] = up[r][c]
+        message(k, 0).start()
+        message(k, 1).start()
+
+    def pack_t(k):
+        tlink = link_rows(7)
+        for s in range(2):
             dn = project(rows_of(k, 0), T, -1, s)
             up = colour(tlink, project(rows_of(k, 7), T, 1, s), True)
             for r in range(2):
                 for c in range(3):
-                    at = pl.ds(8 * r + 3 * s + c, NZ, stride=16)
+                    at = pl.ds(half(r, s, c), NZ, stride=12)
                     st[k, 0, at, :] = dn[r][c] * down_sign
                     st[k, 1, at, :] = up[r][c] * up_sign
+        message(k, 2).start()
+        message(k, 3).start()
 
     def pack_corners(p, k):
-        for m in range(2):
-            for i, (t, sign) in enumerate(((0, down_sign), (7, up_sign))):
-                for r in range(2):
-                    rows = sz[k, m, pl.ds(48 * r + t, 6, stride=8), :]
-                    sr[p, 2 * m + i, pl.ds(8 * r, 6), :] = rows * sign
+        for i, (dz, dt) in enumerate(CORNERS):
+            m = 1 if dt > 0 else 0
+            z = NZ - 1 if dz > 0 else 0
+            sr[p, i, pl.ds(0, 12), :] = st[k, m, pl.ds(12 * z, 12), :]
+            t, sign = (7, up_sign) if dt > 0 else (0, down_sign)
+            sr[p, i, pl.ds(12, 12), :] = sz[k, 1 if dz > 0 else 0, pl.ds(t, 12, stride=8), :] * sign
+            corner(p, i).start()
 
     def message(k, m):
         target = ((-1, 0), (1, 0), (0, -1), (0, 1))[m]
@@ -270,26 +284,17 @@
             device_id=device(*target), device_id_type=MESH,
         )
 
-    def corner(p, k, j):
-        src = (
-            st.at[k, 1, pl.ds(0, 16)], st.at[k, 0, pl.ds(0, 16)],
-            st.at[k, 1, pl.ds(48, 16)], st.at[k, 0, pl.ds(48, 16)],
-            sr.at[p, 2], sr.at[p, 0], sr.at[p, 3], sr.at[p, 1],
-        )[j]
-        target = ((-1, 1), (-1, -1), (1, 1), (1, -1), (1, -1), (-1, -1), (1, 1), (-1, 1))[j]
+    def corner(p, i):
         return pltpu.make_async_remote_copy(
-            src_ref=src, dst_ref=rd.at[p, pl.ds(16 * j, 16)],
-            send_sem=diag_send.at[p, j], recv_sem=diag_recv.at[p, j],
-            device_id=device(*target), device_id_type=MESH,
+            src_ref=sr.at[p, i], dst_ref=rd.at[p, pl.ds(24 * i, 24)],
+            send_sem=diag_send.at[p, i], recv_sem=diag_recv.at[p, i],
+            device_id=device(*CORNERS[i]), device_id_type=MESH,
         )
 
     def corner_link(i):
-        block, target, to = (
-            (0, (-1, 0), 1), (1, (1, 0), 3), (2, (1, 0), 10), (3, (1, 0), 11),
-            (2, (0, -1), 5), (3, (0, 1), 7), (0, (0, 1), 14), (1, (0, 1), 15),
-        )[i]
+        block, count, target, to = ((0, 1, (-1, 0), 0), (1, 3, (1, 0), 1), (2, 1, (0, -1), 4), (3, 3, (0, 1), 5))[i]
         return pltpu.make_async_remote_copy(
-            src_ref=sl.at[block], dst_ref=rl.at[pl.ds(24 * to, 24)],
+            src_ref=sl.at[pl.ds(block, count)], dst_ref=ll.at[pl.ds(to, count)],
             send_sem=link_send.at[i], recv_sem=link_recv.at[i],
             device_id=device(*target), device_id_type=MESH,
         )
@@ -297,8 +302,8 @@
     def finish_t(k):
         link = link_rows(7)
         for s in range(2):
-            a = [[rt[k, 0, pl.ds(8 * r + 3 * s + c, NZ, stride=16), :] for c in range(3)] for r in range(2)]
-            b = [[rt[k, 1, pl.ds(8 * r + 3 * s + c, NZ, stride=16), :] for c in range(3)] for r in range(2)]
+            a = [[rt[k, 0, pl.ds(half(r, s, c), NZ, stride=12), :] for c in range(3)] for r in range(2)]
+            b = [[rt[k, 1, pl.ds(half(r, s, c), NZ, stride=12), :] for c in range(3)] for r in range(2)]
             for w, t, parity in ((colour(link, a, False), 7, 1), (b, 0, -1)):
                 def bump_row(r, s, c, value, sign):
                     at = pl.ds(yrow(k + 1, comp(r, s, c), 0, t), NZ, stride=8)
@@ -318,7 +323,7 @@
             b = [[rz[k, 1, pl.ds(8 * half(r, s, c), 8), :] for c in range(3)] for r in range(2)]
             put_half(k + 1, 0, s, b, -1)
 
-    def correct(p, k):
+    def correct(p):
         one = [rl[pl.ds(e, 8, stride=24), :] for e in range(18)]
         two = [rl[pl.ds(192 + e, 8, stride=24), :] for e in range(18)]
         j = lax.broadcasted_iota(jnp.int32, (8, 128), 0)
@@ -326,7 +331,7 @@
         sign_j = jnp.where(plus, jnp.ones((8, 128), F32), -1.0)
         w = []
         for s in range(2):
-            a = [[rd[p, pl.ds(8 * r + 3 * s + c, 8, stride=16), :] for c in range(3)] for r in range(2)]
+            a = [[rd[p, pl.ds(half(r, s, c), 8, stride=12), :] for c in range(3)] for r in range(2)]
             w.append(colour(one, a, False))
         for s in range(2):
             q = []
@@ -337,87 +342,127 @@
             for r in range(2):
                 for c in range(3):
                     tmp[pl.ds(8 * half(r, s, c), 8), :] = q[r][c]
-        for s in range(2):
+
+    def correct_z(k):
+        for n in range(12):
+            for m in range(2):
+                at = pl.ds(8 * n, 2, stride=7)
+                rz[k, m, at, :] = rz[k, m, at, :] + tmp[pl.ds(8 * n + 4 * m, 2, stride=2), :]
+
+    def correct_t(k):
+        for n in range(12):
+            for m, z, pos in ((0, 0, 7), (0, 3, 3), (1, 0, 5), (1, 3, 1)):
+                at = pl.ds(12 * z + n, 1)
+                rt[k, m, at, :] = rt[k, m, at, :] + tmp[pl.ds(8 * n + pos, 1), :]
+
+    def regroup(n, carry):
+        for c in range(COMPS):
+            f = v[n, pl.ds(c * PLANE, PLANE), :].astype(F32)
+            v[n, pl.ds(c * PLANE, PLANE), :] = jnp.concatenate([f[8:24], f[:8], f[24:]], axis=0).astype(BF16)
+        return carry
+
+    def products(part, h):
+        site = lax.broadcasted_iota(jnp.int32, (16, 128), 1)
+        group = (site >> 6) * 4 + ((site & 15) >> 2)
+        scale = HALF ** 4
+        left = []
+        for c in range(6):
+            rows = []
             for r in range(2):
-                for c in range(3):
-                    n = half(r, s, c)
-                    for m in range(2):
-                        at = pl.ds(8 * n, 2, stride=7)
-                        rz[k, m, at, :] = rz[k, m, at, :] + tmp[pl.ds(8 * n + 2 * m, 2), :]
-                        at = pl.ds(8 * r + 3 * s + c, 2, stride=48)
-                        rt[k, m, at, :] = rt[k, m, at, :] + tmp[pl.ds(8 * n + 4 + 2 * m, 2), :]
+                n = comp(r, 2 * h, 0) + c
+                if part == 0:
+                    field = y[pl.ds(yrow(4, n, 1), 16), :]
+                else:
+                    field = jnp.concatenate([y[pl.ds(yrow(4, n, 0), 8), :], y[pl.ds(yrow(4, n, 3), 8), :]], axis=0)
+                rows.append((field * scale).astype(BF16))
+                left.append(v[:, pl.ds(n * PLANE + 16 * part, 16), :].reshape(VECS * 16, 128))
+            for grp in range(8):
+                keep = (group == grp).astype(F32).astype(BF16)
+                re, im = rows[0] * keep, rows[1] * keep
+                col = 256 * c
+                wt[2 * part + h, pl.ds(16 * grp, 16), col:col + 128] = re
+                wt[2 * part + h, pl.ds(16 * grp, 16), col + 128:col + 256] = im
+                wt[2 * part + h, pl.ds(128 + 16 * grp, 16), col:col + 128] = im
+                wt[2 * part + h, pl.ds(128 + 16 * grp, 16), col + 128:col + 256] = -re
+        return lax.dot_general(
+            jnp.concatenate(left, axis=1), wt[2 * part + h], (((1,), (1,)), ((), ())), preferred_element_type=F32
+        )
 
     loads[0].wait()
     loads[1].wait()
-    for i, (direction, z, t) in enumerate(((T, 0, 7), (T, 3, 7), (Z, 3, 0), (Z, 3, 7))):
+    corner_rows = ((T, 0, 7), (T, 3, 7), (Z, 3, 0), (Z, 3, 7))
+    for i in range(6):
+        direction, z, t = corner_rows[i % 4]
         for e, count in ((0, 8), (8, 8), (16, 2)):
             sl[i, pl.ds(e, count), :] = g[pl.ds((18 * direction + e) * PLANE + z * 8 + t, count, stride=32), :]
-    loads[2].wait()
     pl.semaphore_wait(barrier, len(greet))
 
     for p in range(2):
         k = 2 * p
-        pack(k)
-        for m in range(4):
-            message(k, m).start()
+        pack_z(k)
+        pack_t(k)
         pack_corners(p, k)
-        for j in range(8):
-            corner(p, k, j).start()
         if p == 0:
-            for i in range(8):
+            for i in range(4):
                 corner_link(i).start()
-        local(k, None)
-        pack(k + 1)
-        for m in range(4):
-            message(k + 1, m).start()
+            loads[2].wait()
+            loads[3].wait()
+            loads[4].start()
+            prepare()
+
+        def faces():
+            z_backward(k, NZ - 2)
+            z_forward(k, 0)
+            pack_z(k + 1)
+        local(k, NZ - 1, faces)
+        z_forward(k, 1)
+        z_forward(k, 2)
+        z_backward(k, 0)
+        z_backward(k, 1)
+        pack_t(k + 1)
+        if p == 0:
+            loads[4].wait()
+            lax.fori_loop(0, VECS, regroup, 0)
         message(k, 2).wait_recv()
         message(k, 3).wait_recv()
         finish_t(k)
 
-        def at_third():
+        def halo():
+            z_forward(k + 1, 1)
+            z_backward(k + 1, 1)
             message(k, 0).wait_recv()
             message(k, 1).wait_recv()
             finish_z(k)
-        local(k + 1, at_third)
-        for j in range(8):
-            corner(p, k, j).wait_recv()
+        local(k + 1, 1, halo)
+        z_forward(k + 1, 0)
+        z_forward(k + 1, 2)
+        z_backward(k + 1, 0)
+        z_backward(k + 1, 2)
+        for i in range(4):
+            corner(p, i).wait_recv()
         if p == 0:
-            for i in range(8):
+            for i in range(4):
                 corner_link(i).wait_recv()
-        for m in range(4):
-            message(k + 1, m).wait_recv()
-        correct(p, k + 1)
+            for i, to in enumerate((2, 6, 8 + 4, 8 + 6, 3, 1, 8 + 5, 8 + 1)):
+                rl[pl.ds(24 * to, 24), :] = ll[i]
+        correct(p)
+        message(k + 1, 2).wait_recv()
+        message(k + 1, 3).wait_recv()
+        correct_t(k + 1)
         finish_t(k + 1)
+        if p == 1:
+            for h in range(2):
+                inner[h] = products(0, h)
+        message(k + 1, 0).wait_recv()
+        message(k + 1, 1).wait_recv()
+        correct_z(k + 1)
         finish_z(k + 1)
 
-    loads[3].wait()
-    site = lax.broadcasted_iota(jnp.int32, (16, 128), 1)
-    group = (site >> 6) * 4 + ((site & 15) >> 2)
-    scale = HALF ** 4
     pooled = []
+    i0 = lax.broadcasted_iota(jnp.int32, (VECS * 16, 256), 0) & 15
+    i1 = lax.broadcasted_iota(jnp.int32, (VECS * 16, 256), 1) & 15
     for h in range(2):
-        left = []
-        for zp in range(2):
-            for c in range(6):
-                rows = []
-                for r in range(2):
-                    n = comp(r, 2 * h, 0) + c
-                    rows.append((y[pl.ds(yrow(4, n, 2 * zp), 16), :] * scale).astype(BF16))
-                    left.append(v[:, pl.ds(n * PLANE + 16 * zp, 16), :].reshape(VECS * 16, 128))
-                col = (zp * 6 + c) * 256
-                for grp in range(8):
-                    keep = (group == grp).astype(F32).astype(BF16)
-                    re, im = rows[0] * keep, rows[1] * keep
-                    wt[pl.ds(16 * grp, 16), col:col + 128] = re
-                    wt[pl.ds(16 * grp, 16), col + 128:col + 256] = im
-                    wt[pl.ds(128 + 16 * grp, 16), col:col + 128] = im
-                    wt[pl.ds(128 + 16 * grp, 16), col + 128:col + 256] = -re
-        prod = lax.dot_general(
-            jnp.concatenate(left, axis=1), wt[...], (((1,), (1,)), ((), ())), preferred_element_type=F32
-        )
-        i0 = lax.broadcasted_iota(jnp.int32, (VECS * 16, 256), 0) & 15
-        i1 = lax.broadcasted_iota(jnp.int32, (VECS * 16, 256), 1) & 15
-        prod = jnp.where(i0 == i1, prod, 0.0)
+        prod = jnp.where(i0 == i1, inner[h] + products(1, h), 0.0)
         pooled.append(jnp.sum(prod.reshape(VECS, 16, 256), axis=1))
     zero = jnp.zeros((2 * VECS, 128), F32)
     pooled = jnp.concatenate(pooled, axis=0)
@@ -438,7 +483,7 @@
             device_id=(me_z, to), device_id_type=MESH,
         )
 
-    for d in range(1, TA):
+    for d in FAR_FIRST:
         exchange(d).start()
     mine = pl.ds(pl.multiple_of(8 * me_t, 8), 8)
     rc[mine, :] = so[mine, :]
@@ -461,53 +506,55 @@
         for m in range(4):
             message(2 * p, m).wait_send()
             message(2 * p + 1, m).wait_send()
-        for j in range(8):
-            corner(p, 2 * p, j).wait_send()
-    for i in range(8):
+        for i in range(4):
+            corner(p, i).wait_send()
+    for i in range(4):
         corner_link(i).wait_send()
     write.wait()
 
 
 def on_device(source, gauge_links, clover_term, null_vectors, owners):
-    any_space = pl.BlockSpec(memory_space=pl.ANY)
+    hbm = pl.BlockSpec(memory_space=pltpu.HBM)
     vmem = pl.BlockSpec(memory_space=pltpu.VMEM)
     dma = pltpu.SemaphoreType.DMA
     x, coarse = pl.pallas_call(
         kernel,
         out_shape=(jax.ShapeDtypeStruct((FIELD, 128), F32), jax.ShapeDtypeStruct((128, 128), F32)),
-        in_specs=[any_space, any_space, any_space, any_space, vmem],
-        out_specs=(any_space, vmem),
+        in_specs=[hbm, hbm, hbm, hbm, vmem],
+        out_specs=(pl.BlockSpec(memory_space=pl.ANY), vmem),
         scratch_shapes=[
             pltpu.VMEM((5 * FIELD, 128), F32),
             pltpu.VMEM((72 * PLANE, 128), F32),
             pltpu.VMEM((144 * PLANE, 128), F32),
             pltpu.VMEM((VECS, FIELD, 128), BF16),
             pltpu.VMEM((4, 2, 96, 128), F32),
-            pltpu.VMEM((4, 2, 64, 128), F32),
-            pltpu.VMEM((2, 4, 16, 128), F32),
-            pltpu.VMEM((4, 24, 128), F32),
+            pltpu.VMEM((4, 2, 48, 128), F32),
+            pltpu.VMEM((2, 4, 24, 128), F32),
+            pltpu.VMEM((6, 24, 128), F32),
+            pltpu.VMEM((8, 24, 128), F32),
             pltpu.VMEM((4, 2, 96, 128), F32),
-            pltpu.VMEM((4, 2, 64, 128), F32),
-            pltpu.VMEM((2, 128, 128), F32),
+            pltpu.VMEM((4, 2, 48, 128), F32),
+            pltpu.VMEM((2, 96, 128), F32),
             pltpu.VMEM((16 * 24, 128), F32),
             pltpu.VMEM((96, 128), F32),
-            pltpu.VMEM((256, 3072), BF16),
+            pltpu.VMEM((4, 256, 1536), BF16),
+            pltpu.VMEM((2, VECS * 16, 256), F32),
             pltpu.VMEM((128, 256), F32),
             pltpu.VMEM((128, 128), F32),
             pltpu.VMEM((128, 128), F32),
             pltpu.VMEM((FIELD, 128), F32),
-            dma((4,)), dma((4, 4)), dma((4, 4)), dma((2, 8)), dma((2, 8)),
-            dma((8,)), dma((8,)), dma((TA,)), dma((TA,)), dma,
+            dma((5,)), dma((4, 4)), dma((4, 4)), dma((2, 4)), dma((2, 4)),
+            dma((4,)), dma((4,)), dma((TA,)), dma((TA,)), dma,
         ],
         compiler_params=pltpu.CompilerParams(
-            collective_id=0, has_side_effects=True, vmem_limit_bytes=48 * 1024 * 1024
+            collective_id=0, has_side_effects=True, vmem_limit_bytes=63 * 1024 * 1024
         ),
     )(
         source.reshape(FIELD, 128),
         gauge_links.reshape(72 * PLANE, 128),
         clover_term.reshape(144 * PLANE, 128),
         null_vectors.reshape(VECS, FIELD, 128),
-        owners,
+        owners.reshape(1, 16),
     )
     coarse = coarse.reshape(TA, 8, 128)[:, :2, :4 * VECS].reshape(2 * TA, 4 * VECS).T
     return x.reshape(source.shape), coarse

time: 41.4 us -> 37.7 us (0.911)
  local copies, waits for them, and re-layouts: 6.02 us -> 3.22 us
  Pallas kernels: 34.5 us -> 33.6 us
    unnamed x8 -> x1, local copies, waits for them, and re-layouts: 5.41 us -> 1.77 us
    pallas_call x1, Pallas kernels: 34.5 us -> 33.6 us  [on_device(): pl.pallas_call(kernel, out_shape=(jax.ShapeDtypeStruct((FIELD, 128), F32)...]
    slice x1, local copies, waits for them, and re-layouts: 0.61 us -> 1.45 us  [on_device(): coarse.reshape(TA, 8, 128)[:, :2, :4 * VECS].reshape(2 * TA, 4 * VECS)]
where the time goes in v1:
time: 37.7 us; the launch traced here: 37.5 us
  Pallas kernels  33.6 us (89%)
  local copies, waits for them, and re-layouts  3.22 us (9%)
  between operations  0.64 us (2%)
    pallas_call x1, Pallas kernels, on_device(): pl.pallas_call(kernel, out_shape=(jax.ShapeDtypeStruct((FIELD, 128), F32)...  33.6 us
    unnamed x1, local copies, waits for them, and re-layouts  1.77 us
    slice x1, local copies, waits for them, and re-layouts, on_device(): coarse.reshape(TA, 8, 128)[:, :2, :4 * VECS].reshape(2 * TA, 4 * VECS)  1.45 us

profile of v1, /device:TPU:1, one launch (start us, length us, event | category | flops | bytes accessed | tf_op | source)
XLA Modules:
  0.0 37.5 jit_solution(7380706482174436664)
XLA Ops:
  0.6 33.6 %shard_map.68 = (f32[768,128]{1,0:T(8,128)}, f32[128,128]{1,0:T(8,128)}) custom-call(f32[768,128]{1,0:T(8,128)} %bitcast.13, f32[2304,128]{1,0:T(8,128)} %bitcast.12, f32[4608,128]{1,0:T(8,128)} %bitcast.11, bf16[24,768,128]{2,1,0:T(8,128)(2,1)} %bitcast.10, s32[1,16]{1,0:T(1,128)} %bitcast.17), custom_call_target="tpu_custom_call" | custom-call | tf_op jit(solution)/shard_map/pallas_call | solution.py:520
  34.2 1.4 %slice.4 = f32[16,2,96]{2,1,0:T(2,128)} slice(f32[16,8,128]{2,1,0:T(8,128)} %bitcast.16), slice={[0:16], [0:2], [0:96]} | slice | bytes 24576 | tf_op jit(solution)/shard_map/slice | solution.py:559
  35.7 1.8 %copy.8 = f32[24,4,8,128]{3,2,1,0:T(8,128)} copy(f32[24,4,8,128]{3,2,1,0:T(8,128)} %bitcast.14) | data formatting | bytes 786432

commit v2 on v1

--- a/solution.py
+++ b/solution.py
@@ -88,8 +88,8 @@
 
 def kernel(
     source, links, clover, vectors, owners, x_out, coarse_out,
-    y, g, cl, v, sz, st, sr, sl, ll, rz, rt, rd, rl, tmp, wt, inner, place, so, rc, xs,
-    load_sem, msg_send, msg_recv, diag_send, diag_recv, link_send, link_recv, all_send, all_recv, x_sem,
+    y, g, cl, v, sz, st, sr, sl, ll, rz, rt, rd, rl, tmp, wt, inner, place, so, rc, ow,
+    load_sem, msg_send, msg_recv, diag_send, diag_recv, link_send, link_recv, all_send, all_recv,
 ):
     me_z = lax.axis_index("gz")
     me_t = lax.axis_index("ta")
@@ -98,9 +98,10 @@
         return (lax.rem(me_z + (dz + GZ), GZ), lax.rem(me_t + (dt + TA), TA))
 
     def prepare():
+        loads[5].wait()
         sub = lax.broadcasted_iota(jnp.int32, (16, 128), 0)
         lane = lax.broadcasted_iota(jnp.int32, (16, 128), 1)
-        padded = jnp.concatenate([owners[...].astype(F32), jnp.full((1, 112), -1.0, F32)], axis=1)
+        padded = jnp.concatenate([ow[...].astype(F32), jnp.full((1, 112), -1.0, F32)], axis=1)
         own_row = jnp.broadcast_to(padded, (16, 128))
         own = jnp.sum(jnp.where(sub == lane, own_row, 0.0), axis=1, keepdims=True)
         rank = jnp.sum(jnp.where((own == own_row) & (lane < sub), 1.0, 0.0), axis=1, keepdims=True)
@@ -125,6 +126,7 @@
         pltpu.make_async_copy(links.at[pl.ds(0, half_links)], g.at[pl.ds(0, half_links)], load_sem.at[2]),
         pltpu.make_async_copy(clover, cl, load_sem.at[3]),
         pltpu.make_async_copy(vectors, v, load_sem.at[4]),
+        pltpu.make_async_copy(owners, ow, load_sem.at[5]),
     ]
     for c in loads[:4]:
         c.start()
@@ -408,6 +410,7 @@
             loads[2].wait()
             loads[3].wait()
             loads[4].start()
+            loads[5].start()
             prepare()
 
         def faces():
@@ -493,15 +496,14 @@
         total = y[at[2], :] + HALF * y[at[3], :]
         total = y[at[1], :] + HALF * total
         total = y[at[0], :] + HALF * total
-        xs[at[0], :] = WEIGHT * total
+        x_out[at[0], :] = WEIGHT * total
         return carry
     lax.fori_loop(0, COMPS, solution_rows, 0)
-    write = pltpu.make_async_copy(xs, x_out, x_sem)
-    write.start()
 
     for d in range(1, TA):
         exchange(d).wait()
-    coarse_out[...] = rc[...]
+    for r in range(2):
+        coarse_out[pl.ds(r, TA, stride=2), :] = rc[pl.ds(r, TA, stride=8), :]
     for p in range(2):
         for m in range(4):
             message(2 * p, m).wait_send()
@@ -510,7 +512,10 @@
             corner(p, i).wait_send()
     for i in range(4):
         corner_link(i).wait_send()
-    write.wait()
+
+
+def keep(value):
+    return pltpu.with_memory_space_constraint(value, pltpu.HBM)
 
 
 def on_device(source, gauge_links, clover_term, null_vectors, owners):
@@ -519,9 +524,9 @@
     dma = pltpu.SemaphoreType.DMA
     x, coarse = pl.pallas_call(
         kernel,
-        out_shape=(jax.ShapeDtypeStruct((FIELD, 128), F32), jax.ShapeDtypeStruct((128, 128), F32)),
-        in_specs=[hbm, hbm, hbm, hbm, vmem],
-        out_specs=(pl.BlockSpec(memory_space=pl.ANY), vmem),
+        out_shape=(pltpu.VMEM((FIELD, 128), F32), pltpu.VMEM((2 * TA, 128), F32)),
+        in_specs=[hbm] * 5,
+        out_specs=(vmem, vmem),
         scratch_shapes=[
             pltpu.VMEM((5 * FIELD, 128), F32),
             pltpu.VMEM((72 * PLANE, 128), F32),
@@ -542,22 +547,21 @@
             pltpu.VMEM((128, 256), F32),
             pltpu.VMEM((128, 128), F32),
             pltpu.VMEM((128, 128), F32),
-            pltpu.VMEM((FIELD, 128), F32),
-            dma((5,)), dma((4, 4)), dma((4, 4)), dma((2, 4)), dma((2, 4)),
-            dma((4,)), dma((4,)), dma((TA,)), dma((TA,)), dma,
+            pltpu.VMEM((1, 16), jnp.int32),
+            dma((6,)), dma((4, 4)), dma((4, 4)), dma((2, 4)), dma((2, 4)),
+            dma((4,)), dma((4,)), dma((TA,)), dma((TA,)),
         ],
         compiler_params=pltpu.CompilerParams(
-            collective_id=0, has_side_effects=True, vmem_limit_bytes=63 * 1024 * 1024
+            collective_id=0, has_side_effects=True, vmem_limit_bytes=40 * 1024 * 1024
         ),
     )(
-        source.reshape(FIELD, 128),
-        gauge_links.reshape(72 * PLANE, 128),
-        clover_term.reshape(144 * PLANE, 128),
-        null_vectors.reshape(VECS, FIELD, 128),
-        owners.reshape(1, 16),
+        keep(source.reshape(FIELD, 128)),
+        keep(gauge_links.reshape(72 * PLANE, 128)),
+        keep(clover_term.reshape(144 * PLANE, 128)),
+        keep(null_vectors.reshape(VECS, FIELD, 128)),
+        keep(owners.reshape(1, 16)),
     )
-    coarse = coarse.reshape(TA, 8, 128)[:, :2, :4 * VECS].reshape(2 * TA, 4 * VECS).T
-    return x.reshape(source.shape), coarse
+    return x.reshape(source.shape), coarse[:, :4 * VECS].T
 
 
 def solution(mesh):

time: 37.7 us -> 34.7 us (0.920)
  local copies, waits for them, and re-layouts: 3.22 us -> 1.35 us
  Pallas kernels: 33.6 us -> 32.6 us
    slice x1 -> x0, local copies, waits for them, and re-layouts: 1.45 us -> none  [on_device(): coarse.reshape(TA, 8, 128)[:, :2, :4 * VECS].reshape(2 * TA, 4 * VECS)]
    pallas_call x1, Pallas kernels: 33.6 us -> 32.6 us  [on_device(): pl.pallas_call(kernel, out_shape=(pltpu.VMEM((FIELD, 128), F32), pltpu.VM...]
    unnamed x1, local copies, waits for them, and re-layouts: 1.77 us -> 0.75 us
    transpose x0 -> x1, local copies, waits for them, and re-layouts: none -> 0.61 us  [on_device(): return (x.reshape(source.shape), coarse[:, :4 * VECS].T)]
where the time goes in v2:
time: 34.7 us; the launch traced here: 34.6 us
  Pallas kernels  32.6 us (94%)
  local copies, waits for them, and re-layouts  1.35 us (4%)
  between operations  0.64 us (2%)
    pallas_call x1, Pallas kernels, on_device(): pl.pallas_call(kernel, out_shape=(pltpu.VMEM((FIELD, 128), F32), pltpu.VM...  32.6 us
    unnamed x1, local copies, waits for them, and re-layouts  0.75 us

profile of v2, /device:TPU:1, one launch (start us, length us, event | category | flops | bytes accessed | tf_op | source)
XLA Modules:
  0.0 34.6 jit_solution(17476293011841578076)
XLA Ops:
  0.6 32.6 %shard_map.68 = (f32[768,128]{1,0:T(8,128)S(1)}, f32[32,128]{1,0:T(8,128)S(1)}) custom-call(f32[768,128]{1,0:T(8,128)} %bitcast.12, f32[2304,128]{1,0:T(8,128)} %bitcast.11, f32[4608,128]{1,0:T(8,128)} %bitcast.10, bf16[24,768,128]{2,1,0:T(8,128)(2,1)} %bitcast.9, s32[1,16]{1,0:T(1,128)} %bitcast.13), custom_call_target="tpu_custom_call" | custom-call | tf_op jit(solution)/shard_map/pallas_call | solution.py:525
  33.2 0.7 %copy.8 = f32[24,4,8,128]{3,2,1,0:T(8,128)} copy(f32[24,4,8,128]{3,2,1,0:T(8,128)S(1)} %bitcast.8) | data formatting | bytes 786432
  34.0 0.6 %slice_bitcast_fusion = f32[96,32]{0,1:T(8,128)} fusion(f32[32,128]{1,0:T(8,128)S(1)} %get-tuple-element.5), kind=kLoop, calls=%fused_computation | loop fusion | bytes 24576 | tf_op jit(solution)/shard_map/transpose | solution.py:564

commit v3 on v2

--- a/solution.py
+++ b/solution.py
@@ -32,6 +32,7 @@
 INVERSE = {X: -1, Y: -1, Z: -1, T: 1}
 
 
+LINK_ROWS = ((0, (0,)), (24, (1, 2, 3)), (80, (2,)), (104, (3, 0, 1)))
 NEAR_FIRST = (1, 15, 2, 14, 3, 13, 4, 12, 5, 11, 6, 10, 7, 9, 8)
 FAR_FIRST = (8, 7, 9, 6, 10, 5, 11, 4, 12, 3, 13, 2, 14, 1, 15)
 
@@ -110,7 +111,9 @@
             agg = ((lane & 7) >> 2) * 8 + ((lane >> 4) & 7)
             of_lane = jnp.sum(jnp.where(agg == sub, slot, 0.0), axis=0, keepdims=True)
             row = lax.broadcasted_iota(jnp.int32, (128, 128), 0).astype(F32)
-            place[:, 128 * part:128 * (part + 1)] = jnp.where(row == of_lane, 1.0, 0.0)
+            ones = jnp.where(row == of_lane, 1.0, 0.0).astype(BF16)
+            for copy in range(3):
+                place[:, 256 * copy + 128 * part:256 * copy + 128 * (part + 1)] = ones
 
         for j in range(16):
             for e in (0, 8, 16):
@@ -128,7 +131,7 @@
         pltpu.make_async_copy(vectors, v, load_sem.at[4]),
         pltpu.make_async_copy(owners, ow, load_sem.at[5]),
     ]
-    for c in loads[:4]:
+    for c in loads[:4] + loads[5:]:
         c.start()
 
     barrier = pltpu.get_barrier_semaphore()
@@ -294,9 +297,10 @@
         )
 
     def corner_link(i):
-        block, count, target, to = ((0, 1, (-1, 0), 0), (1, 3, (1, 0), 1), (2, 1, (0, -1), 4), (3, 3, (0, 1), 5))[i]
+        target = ((-1, 0), (1, 0), (0, -1), (0, 1))[i]
+        at = pl.ds(LINK_ROWS[i][0], 24 if len(LINK_ROWS[i][1]) == 1 else 56)
         return pltpu.make_async_remote_copy(
-            src_ref=sl.at[pl.ds(block, count)], dst_ref=ll.at[pl.ds(to, count)],
+            src_ref=sl.at[at], dst_ref=ll.at[at],
             send_sem=link_send.at[i], recv_sem=link_recv.at[i],
             device_id=device(*target), device_id_type=MESH,
         )
@@ -392,11 +396,6 @@
 
     loads[0].wait()
     loads[1].wait()
-    corner_rows = ((T, 0, 7), (T, 3, 7), (Z, 3, 0), (Z, 3, 7))
-    for i in range(6):
-        direction, z, t = corner_rows[i % 4]
-        for e, count in ((0, 8), (8, 8), (16, 2)):
-            sl[i, pl.ds(e, count), :] = g[pl.ds((18 * direction + e) * PLANE + z * 8 + t, count, stride=32), :]
     pl.semaphore_wait(barrier, len(greet))
 
     for p in range(2):
@@ -405,13 +404,17 @@
         pack_t(k)
         pack_corners(p, k)
         if p == 0:
+            corner_rows = ((T, 0, 7), (T, 3, 7), (Z, 3, 0), (Z, 3, 7))
+            for base, blocks in LINK_ROWS:
+                for n, b in enumerate(blocks):
+                    direction, z, t = corner_rows[b]
+                    rows = g[pl.ds((18 * direction) * PLANE + z * 8 + t, 18, stride=32), :]
+                    sl[pl.ds(base + 18 * n, 18), :] = rows
             for i in range(4):
                 corner_link(i).start()
             loads[2].wait()
             loads[3].wait()
             loads[4].start()
-            loads[5].start()
-            prepare()
 
         def faces():
             z_backward(k, NZ - 2)
@@ -424,6 +427,7 @@
         z_backward(k, 1)
         pack_t(k + 1)
         if p == 0:
+            prepare()
             loads[4].wait()
             lax.fori_loop(0, VECS, regroup, 0)
         message(k, 2).wait_recv()
@@ -446,8 +450,9 @@
         if p == 0:
             for i in range(4):
                 corner_link(i).wait_recv()
-            for i, to in enumerate((2, 6, 8 + 4, 8 + 6, 3, 1, 8 + 5, 8 + 1)):
-                rl[pl.ds(24 * to, 24), :] = ll[i]
+            for (base, _), slots in zip(LINK_ROWS, ((2,), (6, 12, 14), (3,), (1, 13, 9))):
+                for n, to in enumerate(slots):
+                    rl[pl.ds(24 * to, 18), :] = ll[pl.ds(base + 18 * n, 18), :]
         correct(p)
         message(k + 1, 2).wait_recv()
         message(k + 1, 3).wait_recv()
@@ -472,9 +477,13 @@
     first = jnp.concatenate([pooled[:, :128], zero], axis=1)
     second = jnp.concatenate([zero, pooled[:, 128:]], axis=1)
     values = jnp.concatenate([first, second, jnp.zeros((32, 256), F32)], axis=0)
+    high = values.astype(BF16)
+    rest = values - high.astype(F32)
+    middle = rest.astype(BF16)
+    low = (rest - middle.astype(F32)).astype(BF16)
     so[...] = lax.dot_general(
-        place[...], values, (((1,), (1,)), ((), ())), preferred_element_type=F32,
-        precision=lax.Precision.HIGHEST,
+        place[...], jnp.concatenate([high, middle, low], axis=1), (((1,), (1,)), ((), ())),
+        preferred_element_type=F32,
     )
 
     def exchange(d):
@@ -535,8 +544,8 @@
             pltpu.VMEM((4, 2, 96, 128), F32),
             pltpu.VMEM((4, 2, 48, 128), F32),
             pltpu.VMEM((2, 4, 24, 128), F32),
-            pltpu.VMEM((6, 24, 128), F32),
-            pltpu.VMEM((8, 24, 128), F32),
+            pltpu.VMEM((160, 128), F32),
+            pltpu.VMEM((160, 128), F32),
             pltpu.VMEM((4, 2, 96, 128), F32),
             pltpu.VMEM((4, 2, 48, 128), F32),
             pltpu.VMEM((2, 96, 128), F32),
@@ -544,7 +553,7 @@
             pltpu.VMEM((96, 128), F32),
             pltpu.VMEM((4, 256, 1536), BF16),
             pltpu.VMEM((2, VECS * 16, 256), F32),
-            pltpu.VMEM((128, 256), F32),
+            pltpu.VMEM((128, 768), BF16),
             pltpu.VMEM((128, 128), F32),
             pltpu.VMEM((128, 128), F32),
             pltpu.VMEM((1, 16), jnp.int32),

time: 34.7 us -> 34.2 us (0.986)
  Pallas kernels: 32.6 us -> 32 us
    pallas_call x1, Pallas kernels: 32.6 us -> 32 us  [on_device(): pl.pallas_call(kernel, out_shape=(pltpu.VMEM((FIELD, 128), F32), pltpu.VM...]
where the time goes in v3:
time: 34.2 us; the launch traced here: 34 us
  Pallas kernels  32 us (94%)
  local copies, waits for them, and re-layouts  1.35 us (4%)
  between operations  0.64 us (2%)
    pallas_call x1, Pallas kernels, on_device(): pl.pallas_call(kernel, out_shape=(pltpu.VMEM((FIELD, 128), F32), pltpu.VM...  32 us
    unnamed x1, local copies, waits for them, and re-layouts  0.75 us

profile of v3, /device:TPU:1, one launch (start us, length us, event | category | flops | bytes accessed | tf_op | source)
XLA Modules:
  0.0 34.0 jit_solution(13650246988132632703)
XLA Ops:
  0.6 32.0 %shard_map.68 = (f32[768,128]{1,0:T(8,128)S(1)}, f32[32,128]{1,0:T(8,128)S(1)}) custom-call(f32[768,128]{1,0:T(8,128)} %bitcast.12, f32[2304,128]{1,0:T(8,128)} %bitcast.11, f32[4608,128]{1,0:T(8,128)} %bitcast.10, bf16[24,768,128]{2,1,0:T(8,128)(2,1)} %bitcast.9, s32[1,16]{1,0:T(1,128)} %bitcast.13), custom_call_target="tpu_custom_call" | custom-call | tf_op jit(solution)/shard_map/pallas_call | solution.py:534
  32.7 0.7 %copy.8 = f32[24,4,8,128]{3,2,1,0:T(8,128)} copy(f32[24,4,8,128]{3,2,1,0:T(8,128)S(1)} %bitcast.8) | data formatting | bytes 786432
  33.4 0.6 %slice_bitcast_fusion = f32[96,32]{0,1:T(8,128)} fusion(f32[32,128]{1,0:T(8,128)S(1)} %get-tuple-element.5), kind=kLoop, calls=%fused_computation | loop fusion | bytes 24576 | tf_op jit(solution)/shard_map/transpose | solution.py:573

commit v4 on v3

--- a/solution.py
+++ b/solution.py
@@ -537,20 +537,20 @@
         in_specs=[hbm] * 5,
         out_specs=(vmem, vmem),
         scratch_shapes=[
-            pltpu.VMEM((5 * FIELD, 128), F32),
-            pltpu.VMEM((72 * PLANE, 128), F32),
+            pltpu.VMEM((5 * FIELD + 64, 128), F32),
+            pltpu.VMEM((80 * PLANE, 128), F32),
             pltpu.VMEM((144 * PLANE, 128), F32),
             pltpu.VMEM((VECS, FIELD, 128), BF16),
-            pltpu.VMEM((4, 2, 96, 128), F32),
-            pltpu.VMEM((4, 2, 48, 128), F32),
+            pltpu.VMEM((5, 2, 96, 128), F32),
+            pltpu.VMEM((5, 2, 48, 128), F32),
             pltpu.VMEM((2, 4, 24, 128), F32),
-            pltpu.VMEM((160, 128), F32),
-            pltpu.VMEM((160, 128), F32),
-            pltpu.VMEM((4, 2, 96, 128), F32),
-            pltpu.VMEM((4, 2, 48, 128), F32),
+            pltpu.VMEM((176, 128), F32),
+            pltpu.VMEM((176, 128), F32),
+            pltpu.VMEM((5, 2, 96, 128), F32),
+            pltpu.VMEM((5, 2, 48, 128), F32),
             pltpu.VMEM((2, 96, 128), F32),
             pltpu.VMEM((16 * 24, 128), F32),
-            pltpu.VMEM((96, 128), F32),
+            pltpu.VMEM((160, 128), F32),
             pltpu.VMEM((4, 256, 1536), BF16),
             pltpu.VMEM((2, VECS * 16, 256), F32),
             pltpu.VMEM((128, 768), BF16),

time: 34.2 us -> 34.2 us (level)
  no operation moved by 1% of the time
where the time goes in v4:
time: 34.2 us; the launch traced here: 34 us
  Pallas kernels  32 us (94%)
  local copies, waits for them, and re-layouts  1.35 us (4%)
  between operations  0.64 us (2%)
    pallas_call x1, Pallas kernels, on_device(): pl.pallas_call(kernel, out_shape=(pltpu.VMEM((FIELD, 128), F32), pltpu.VM...  32 us
    unnamed x1, local copies, waits for them, and re-layouts  0.75 us

profile of v4, /device:TPU:1, one launch (start us, length us, event | category | flops | bytes accessed | tf_op | source)
XLA Modules:
  0.0 34.0 jit_solution(382433886969886762)
XLA Ops:
  0.6 32.0 %shard_map.68 = (f32[768,128]{1,0:T(8,128)S(1)}, f32[32,128]{1,0:T(8,128)S(1)}) custom-call(f32[768,128]{1,0:T(8,128)} %bitcast.12, f32[2304,128]{1,0:T(8,128)} %bitcast.11, f32[4608,128]{1,0:T(8,128)} %bitcast.10, bf16[24,768,128]{2,1,0:T(8,128)(2,1)} %bitcast.9, s32[1,16]{1,0:T(1,128)} %bitcast.13), custom_call_target="tpu_custom_call" | custom-call | tf_op jit(solution)/shard_map/pallas_call | solution.py:534
  32.7 0.7 %copy.8 = f32[24,4,8,128]{3,2,1,0:T(8,128)} copy(f32[24,4,8,128]{3,2,1,0:T(8,128)S(1)} %bitcast.8) | data formatting | bytes 786432
  33.4 0.6 %slice_bitcast_fusion = f32[96,32]{0,1:T(8,128)} fusion(f32[32,128]{1,0:T(8,128)S(1)} %get-tuple-element.5), kind=kLoop, calls=%fused_computation | loop fusion | bytes 24576 | tf_op jit(solution)/shard_map/transpose | solution.py:573
